TPU v7x, 32 devices: a whole 2x2x4 slice. The times are simulated.
32 devices in a mesh: group: 4 (over y, core), space: 8 (over z, x).
Axes of the slice: x: 2, y: 2, z: 4, core: 2. Of those that a mesh axis runs over, the one named last changes fastest.
Arguments:
- initial_state: float32 [32, 3, 32, 1024], P(('group', 'space')), may hold values from -3 to 3
- phases: int32 [32, 32, 1024], P(('group', 'space')), may hold values from 0 to 2
- brick_coords: int32 [32, 3], P(('group', 'space')), may hold values from -1 to 7, as said below
- neighbours: int32 [32, 6], P(('group', 'space')), may hold values from -1 to 31, as said below
- source: float32 [32, 3, 32, 1024], P(('group', 'space'))
- coarse_inverse: float32 [4, 24, 24], P('group', 'space')
Outputs:
- final_state: float32 [32, 3, 32, 1024], P(('group', 'space'))
Inputs may be any that keep to these rules, and one draw needn't show every extreme that they name: `brick_coords`: an occupied slot of device (g, s) holds the brick at x place bx, y = s, z = g; each x place occurs at most once on a device; an empty slot is -1 in all three; device (0, 0), every device with s = 7, and device (3, 6) have every slot occupied. Global slot = device index (group index * 8 + space index) + slot. The -x and +x neighbours lie on the same device, -y and +y on the device one step lower or higher along space, -z and +z one step lower or higher along group, always at the same x place; a face has a neighbour exactly where that brick is occupied; the relation is symmetric; empty slots have -1 everywhere.
All inputs are finite; a program needn't handle non-finite values.
Results may differ from a plain program's by a relative error of at most 0.0003.
Values sent between devices are 32-bit elements; how exact they have to be, the bound alone decides.
A program may use at most 64 MiB of HBM per device.

v0:
```python
import functools

import jax
import jax.numpy as jnp
from jax import lax
from jax.experimental import pallas as pl
from jax.experimental.pallas import tpu as pltpu
from jax.sharding import PartitionSpec as P

NEWTON = 2
SMOOTH = 4
ROUNDS = SMOOTH + 1
E = 32
TILES = 8
PAD = 8
OMEGA = 0.8
MESH = pl.DeviceIdType.MESH
F32 = jnp.float32


def roll(x, shift):
    shift = shift % 128
    return x if shift == 0 else pltpu.roll(x, shift, 1)


def place(f, t):
    return (0, 16 * f + 2 * t) if f < 2 else (1, 2 * t)


def kernel(
    n, m,
    coords, links, inverse, state_in, phase_in, source_in, out,
    state, upd, base, gain, mix, diag, source, phase,
    send, recv, squares_a, squares_b, coarse, weights,
    face_send, face_recv, a_send, a_recv, b_send, b_recv, c_send, c_recv,
):
    me_s = lax.axis_index("space")
    me_g = lax.axis_index("group")
    lane = lax.broadcasted_iota(jnp.int32, (E, 128), 1)
    block = lane // 32
    depth = lane % 32
    first = depth == 0
    last = depth == 31
    edge = first | last
    even = lane % 2 == 0

    targets = (("space", me_s, 1, n), ("space", me_s, -1, n), ("group", me_g, 1, m), ("group", me_g, -1, m))

    def has(axis, me, step, size):
        return me + step < size if step > 0 else me + step >= 0

    barrier = pltpu.get_barrier_semaphore()
    for axis, me, size in (("space", me_s, n), ("group", me_g, m)):
        for d in range(1, size):
            pl.semaphore_signal(barrier, inc=1, device_id={axis: lax.rem(me + d, size)}, device_id_type=MESH)

    def face_copy(r, d):
        axis, me, step, size = targets[d]
        return pltpu.make_async_remote_copy(
            src_ref=send.at[r, d], dst_ref=recv.at[r, d],
            send_sem=face_send.at[r, d], recv_sem=face_recv.at[r, d],
            device_id={axis: jnp.clip(me + step, 0, size - 1)}, device_id_type=MESH)

    def source_of(d):
        axis, me, step, size = targets[d]
        return has(axis, me, -step, size)

    def start_faces(r):
        for d in range(4):
            @pl.when(has(*targets[d]))
            def _():
                face_copy(r, d).start()

    def wait_faces(r):
        for d in range(4):
            @pl.when(source_of(d))
            def _():
                face_copy(r, d).wait_recv()

    def gather_copy(buf, ss, rs, k, d, axis, me, size):
        return pltpu.make_async_remote_copy(
            src_ref=buf.at[k, 0], dst_ref=buf.at[k, d],
            send_sem=ss.at[k, d], recv_sem=rs.at[k, d],
            device_id={axis: lax.rem(me + d, size)}, device_id_type=MESH)

    over_a = (squares_a, a_send, a_recv)
    over_b = (squares_b, b_send, b_recv)
    over_c = (coarse, c_send, c_recv)

    def gather_start(bufs, k, axis, me, size):
        for d in range(1, size):
            gather_copy(*bufs, k, d, axis, me, size).start()

    def gather_wait(bufs, k, axis, me, size):
        for d in range(1, size):
            gather_copy(*bufs, k, d, axis, me, size).wait_recv()


    def swap4(a):
        low = block < 2
        t0 = jnp.where(low, a[0], roll(a[2], 64))
        t2 = jnp.where(low, roll(a[0], 64), a[2])
        t1 = jnp.where(low, a[1], roll(a[3], 64))
        t3 = jnp.where(low, roll(a[1], 64), a[3])
        ev = block % 2 == 0
        return (jnp.where(ev, t0, roll(t1, 32)), jnp.where(ev, roll(t0, 96), t1),
                jnp.where(ev, t2, roll(t3, 32)), jnp.where(ev, roll(t2, 96), t3))

    def spread_in(load):
        tiles = [None] * 8
        for h in range(2):
            got = swap4([load(2 * k + h) for k in range(4)])
            for r in range(4):
                tiles[4 * h + r] = got[r]
        return tiles

    occupied = coords[0, 0] >= 0
    mask = jnp.where(occupied, 1.0, 0.0).astype(F32)
    wall = coords[0, 0].astype(F32) + coords[0, 1].astype(F32) / n + coords[0, 2].astype(F32) / m - 1.0
    linked = [links[0, 2 + d] >= 0 for d in range(4)]

    zero_rows = jnp.zeros((PAD, 128), F32)
    for f in range(3):
        for t in range(TILES):
            edge_rows = zero_rows if f < 2 else zero_rows + wall
            state[f, t, 0:PAD] = edge_rows
            state[f, t, PAD + E:] = edge_rows
            for b in range(2):
                upd[b, f, t, 0:PAD] = zero_rows
                upd[b, f, t, PAD + E:] = zero_rows
    for f in range(3):
        tiles = spread_in(lambda t: state_in[f, :, t * 128:(t + 1) * 128])
        for t in range(TILES):
            state[f, t, PAD:PAD + E] = tiles[t] * mask

    def pack_z(planes, f, t, c):
        q, j = place(f, t)
        part = roll(jnp.where(edge, c, 0.0), j)
        planes[q] = part if planes[q] is None else planes[q] + part

    def post_faces(r, planes, ends):
        q0, q1 = planes
        send[r, 3] = jnp.where(even, q0, roll(q1, 1))
        send[r, 2] = jnp.where(even, roll(q1, -1), q0)
        up = jnp.where(block == 0, roll(ends[0][1], -96), jnp.where(block == 1, roll(ends[1][1], -64), roll(ends[2][1], -32)))
        down = jnp.where(block == 0, ends[0][0], jnp.where(block == 1, roll(ends[1][0], 32), roll(ends[2][0], 64)))
        send[r, 0] = up
        send[r, 1] = down
        start_faces(r)

    def ghosts_of(r, walls):
        wait_faces(r)
        got = [recv[r, d] for d in range(4)]
        y_low, y_high, z_low, z_high = got
        if walls:
            plain = [jnp.where(linked[d], got[d], 0.0) for d in range(4)]
            solid = [jnp.where(linked[d], got[d], wall) for d in range(4)]
        else:
            plain = solid = got
        c0 = jnp.where(even, plain[3], roll(plain[2], 66))
        c1 = jnp.where(even, roll(solid[3], -1), roll(solid[2], 67))
        lows = [roll((plain if f < 2 else solid)[0], -32 * f) for f in range(3)]
        highs = [roll((plain if f < 2 else solid)[1], 96 - 32 * f) for f in range(3)]
        return (c0, c1), lows, highs

    def around(ref, f, t, ghosts):
        planes, lows, highs = ghosts
        c = ref[f, t, PAD:PAD + E]
        total = ref[f, t, PAD - 1:PAD - 1 + E] + ref[f, t, PAD + 1:PAD + 1 + E]
        if t > 0:
            total = total + ref[f, t - 1, PAD:PAD + E]
        else:
            total = total + jnp.where(block == 0, lows[f], roll(ref[f, TILES - 1, PAD:PAD + E], 32))
        if t < TILES - 1:
            total = total + ref[f, t + 1, PAD:PAD + E]
        else:
            total = total + jnp.where(block == 3, highs[f], roll(ref[f, 0, PAD:PAD + E], -32))
        q, j = place(f, t)
        ghost = roll(planes[q], 31 - j)
        total = total + jnp.where(last, ghost, roll(c, -1)) + jnp.where(first, ghost, roll(c, 1))
        return c, total

    def post_state(r):
        planes, ends = [None, None], []
        for f in range(3):
            tiles = [state[f, t, PAD:PAD + E] for t in range(TILES)]
            for t in range(TILES):
                pack_z(planes, f, t, tiles[t])
            ends.append((tiles[0], tiles[TILES - 1]))
        post_faces(r, planes, ends)

    pl.semaphore_wait(barrier, n + m - 2)
    post_state(0)

    rows8 = lax.broadcasted_iota(jnp.int32, (8, 128), 0)
    blank = jnp.zeros((E, 128), F32)
    for d in range(4):
        @pl.when(jnp.logical_not(source_of(d)))
        def _():
            for r in range(NEWTON * ROUNDS):
                recv[r, d] = blank
    for f in range(3):
        tiles = spread_in(lambda t: source_in[f, :, t * 128:(t + 1) * 128])
        for t in range(TILES):
            source[f, t] = tiles[t]
    tiles = spread_in(lambda t: phase_in[:, t * 128:(t + 1) * 128])
    for t in range(TILES):
        phase[t] = tiles[t]
    for d in range(n):
        owner = lax.rem(me_s - d + n, n)
        for i in range(3):
            v = [inverse[0, i, 3 * owner + f] for f in range(3)]
            weights[i, d] = jnp.where(rows8 == 0, v[0], jnp.where(rows8 == 1, v[1], jnp.where(rows8 == 2, v[2], 0.0)))

    def fold(x):
        return x[0:8] + x[8:16] + x[16:24] + x[24:32]

    def sweep(k, carry):
        r0 = k * ROUNDS
        ghosts = ghosts_of(r0, True)
        planes, ends = [None, None], [[None, None] for _ in range(3)]
        square = jnp.zeros((E, 128), F32)
        for t in range(TILES):
            label = phase[t]
            pore = label == 0
            active = label == 1
            conduct = (jnp.where(pore, 1.0, 0.2), jnp.where(pore, 1.0, 0.1),
                       jnp.where(pore, 0.05, jnp.where(active, 0.5, 1.5)))
            rates = jnp.where(pore, 0.0, jnp.where(active, 0.3, 0.02))
            pairs = [around(state, f, t, ghosts) for f in range(3)]
            c, e, s = (p[0] for p in pairs)
            eta = s - e - 0.5 * c
            forward = jnp.exp(0.5 * eta)
            backward = jnp.exp(-0.5 * eta)
            current = rates * (forward - backward)
            slope = 0.5 * rates * (forward + backward)
            react = (-0.5 * current, -current, current)
            for f in range(3):
                v, total = pairs[f]
                misfit = mask * (0.5 * v + conduct[f] * (6.0 * v - total) + react[f] - source[f, t])
                square = square + misfit * misfit
                dg = 0.5 + 6.0 * conduct[f] + (0.25 * slope if f == 0 else slope)
                w = (OMEGA * mask) / dg
                b = -w * misfit
                base[f, t] = b
                upd[0, f, t, PAD:PAD + E] = b
                gain[f, t] = w * conduct[f]
                mix[f, t] = w * slope * (0.5 if f == 0 else 1.0)
                diag[f, t] = dg * (1.0 / OMEGA)
                pack_z(planes, f, t, b)
                if t == 0:
                    ends[f][0] = b
                if t == TILES - 1:
                    ends[f][1] = b
        post_faces(r0 + 1, planes, ends)
        squares_a[k, 0] = fold(square)
        gather_start(over_a, k, "space", me_s, n)

        def terms(u, t, ghosts):
            pairs = [around(u, f, t, ghosts) for f in range(3)]
            c, e, s = (p[0] for p in pairs)
            half = 0.5 * c
            cross = (s - e, s - half, e + half)
            return [(pairs[f][0], base[f, t] + gain[f, t] * pairs[f][1] + mix[f, t] * cross[f]) for f in range(3)]

        def smooth(p, carry):
            now = lax.rem(p, 2)
            u, later = upd.at[now], upd.at[1 - now]
            ghosts = ghosts_of(r0 + 1 + p, False)
            planes, ends = [None, None], [[None, None] for _ in range(3)]
            for t in range(TILES):
                for f, (v, term) in enumerate(terms(u, t, ghosts)):
                    value = (1.0 - OMEGA) * v + term
                    later[f, t, PAD:PAD + E] = value
                    pack_z(planes, f, t, value)
                    if t == 0:
                        ends[f][0] = value
                    if t == TILES - 1:
                        ends[f][1] = value
            post_faces(r0 + 2 + p, planes, ends)
            return carry

        lax.fori_loop(0, 1, smooth, 0)
        gather_wait(over_a, k, "space", me_s, n)
        part = squares_a[k, 0]
        for d in range(1, n):
            part = part + squares_a[k, d]
        squares_b[k, 0] = part
        gather_start(over_b, k, "group", me_g, m)
        lax.fori_loop(1, SMOOTH - 1, smooth, 0)

        u = upd.at[(SMOOTH - 1) % 2]
        ghosts = ghosts_of(r0 + SMOOTH, False)
        sums = [jnp.zeros((E, 128), F32) for _ in range(3)]
        for t in range(TILES):
            for f, (v, term) in enumerate(terms(u, t, ghosts)):
                sums[f] = sums[f] + diag[f, t] * (term - OMEGA * v)
        rows = [jnp.sum(x, axis=0, keepdims=True) for x in sums]
        coarse[k, 0] = jnp.where(rows8 == 0, rows[0], jnp.where(rows8 == 1, rows[1], jnp.where(rows8 == 2, rows[2], 0.0)))
        gather_start(over_c, k, "space", me_s, n)

        gather_wait(over_b, k, "group", me_g, m)
        part = squares_b[k, 0]
        for d in range(1, m):
            part = part + squares_b[k, d]
        whole = jnp.sum(jnp.sum(part, axis=0, keepdims=True), axis=1, keepdims=True)
        cells = 3.0 * n * m * E * E * E
        damping = 1.0 / (1.0 + jnp.sqrt(whole / cells + 1e-6))

        gather_wait(over_c, k, "space", me_s, n)
        got = [coarse[k, d] for d in range(n)]
        planes, ends = [None, None], [[None, None] for _ in range(3)]
        for f in range(3):
            acc = got[0] * weights[f, 0]
            for d in range(1, n):
                acc = acc + got[d] * weights[f, d]
            lift = mask * jnp.sum(jnp.sum(acc, axis=0, keepdims=True), axis=1, keepdims=True)
            for t in range(TILES):
                value = state[f, t, PAD:PAD + E] + damping * (u[f, t, PAD:PAD + E] + lift)
                state[f, t, PAD:PAD + E] = value
                pack_z(planes, f, t, value)
                if t == 0:
                    ends[f][0] = value
                if t == TILES - 1:
                    ends[f][1] = value

        @pl.when(k < NEWTON - 1)
        def _():
            post_faces(r0 + ROUNDS, planes, ends)

        return carry

    lax.fori_loop(0, NEWTON, sweep, 0)

    for f in range(3):
        for h in range(2):
            got = swap4([state[f, 4 * h + r, PAD:PAD + E] for r in range(4)])
            for k in range(4):
                t = 2 * k + h
                out[f, :, t * 128:(t + 1) * 128] = got[k]

    for r in range(NEWTON * ROUNDS):
        for d in range(4):
            @pl.when(has(*targets[d]))
            def _():
                face_copy(r, d).wait_send()
    for k in range(NEWTON):
        for bufs, axis, me, size in ((over_a, "space", me_s, n), (over_b, "group", me_g, m), (over_c, "space", me_s, n)):
            for d in range(1, size):
                gather_copy(*bufs, k, d, axis, me, size).wait_send()


def shards(n, m, initial_state, phases, brick_coords, neighbours, source, coarse_inverse):
    rounds = NEWTON * ROUNDS
    smem = pl.BlockSpec(memory_space=pltpu.SMEM)
    vmem = pl.BlockSpec(memory_space=pltpu.VMEM)
    padded = (3, TILES, E + 2 * PAD, 128)
    inner = (3, TILES, E, 128)
    dma = pltpu.SemaphoreType.DMA
    result = pl.pallas_call(
        functools.partial(kernel, n, m),
        out_shape=jax.ShapeDtypeStruct((3, E, E * E), F32),
        in_specs=[smem, smem, smem, vmem, vmem, vmem],
        out_specs=vmem,
        scratch_shapes=[
            pltpu.VMEM(padded, F32),
            pltpu.VMEM((2,) + padded, F32),
            pltpu.VMEM(inner, F32),
            pltpu.VMEM(inner, F32),
            pltpu.VMEM(inner, F32),
            pltpu.VMEM(inner, F32),
            pltpu.VMEM(inner, F32),
            pltpu.VMEM(inner[1:], jnp.int32),
            pltpu.VMEM((rounds, 4, E, 128), F32),
            pltpu.VMEM((rounds, 4, E, 128), F32),
            pltpu.VMEM((NEWTON, n, 8, 128), F32),
            pltpu.VMEM((NEWTON, m, 8, 128), F32),
            pltpu.VMEM((NEWTON, n, 8, 128), F32),
            pltpu.VMEM((3, n, 8, 128), F32),
            dma((rounds, 4)), dma((rounds, 4)),
            dma((NEWTON, n)), dma((NEWTON, n)),
            dma((NEWTON, m)), dma((NEWTON, m)),
            dma((NEWTON, n)), dma((NEWTON, n)),
        ],
        compiler_params=pltpu.CompilerParams(
            collective_id=0, has_side_effects=True, vmem_limit_bytes=40 * 1024 * 1024
        ),
    )(brick_coords, neighbours, coarse_inverse, initial_state[0], phases[0], source[0])
    return result[None]


def solution(mesh):
    both = ("group", "space")
    return jax.shard_map(
        functools.partial(shards, mesh.shape["space"], mesh.shape["group"]),
        mesh=mesh,
        in_specs=(
            P(both, None, None, None),
            P(both, None, None),
            P(both, None),
            P(both, None),
            P(both, None, None, None),
            P("group", "space", None),
        ),
        out_specs=P(both, None, None, None),
        check_vma=False,
    )
```

profile of v0, /device:TPU:0, one launch (start us, length us, event | category | flops | bytes accessed | tf_op | source)
XLA Modules:
  0.0 62.1 jit_solution(8325769919930763788)
XLA Ops:
  0.0 0.0 copy-start.5
  0.0 0.7 %copy-done.5 = f32[1,3,24]{2,0,1:T(1,128)S(1)} copy-done((f32[1,3,24]{2,0,1:T(1,128)S(1)}, f32[1,3,24]{2,0,1:T(1,128)}, u32[]{:S(2)}) %copy-start.5) | copy-done | bytes 312
  0.7 0.0 copy-start.3
  0.7 0.0 copy-start.4
  0.7 0.6 %copy-done.3 = s32[1,3]{1,0:T(1,128)S(1)} copy-done((s32[1,3]{1,0:T(1,128)S(1)}, s32[1,3]{1,0:T(1,128)}, u32[]{:S(2)}) %copy-start.3) | copy-done | bytes 36
  1.3 0.0 copy-done.4
  1.4 0.0 copy-start
  1.4 1.0 %copy-done = f32[1,3,32,1024]{3,2,1,0:T(8,128)S(1)} copy-done((f32[1,3,32,1024]{3,2,1,0:T(8,128)S(1)}, f32[1,3,32,1024]{3,2,1,0:T(8,128)}, u32[]{:S(2)}) %copy-start) | copy-done | bytes 393240
  2.3 0.0 copy-start.1
  2.4 1.0 %copy-done.1 = f32[1,3,32,1024]{3,2,1,0:T(8,128)S(1)} copy-done((f32[1,3,32,1024]{3,2,1,0:T(8,128)S(1)}, f32[1,3,32,1024]{3,2,1,0:T(8,128)}, u32[]{:S(2)}) %copy-start.1) | copy-done | bytes 393240
  3.3 0.0 copy-start.2
  3.3 0.9 %copy-done.2 = s32[1,32,1024]{2,1,0:T(8,128)S(1)} copy-done((s32[1,32,1024]{2,1,0:T(8,128)S(1)}, s32[1,32,1024]{2,1,0:T(8,128)}, u32[]{:S(2)}) %copy-start.2) | copy-done | bytes 131096
  4.3 57.1 %shard_map.64 = f32[3,32,1024]{2,1,0:T(8,128)S(1)} custom-call(s32[1,3]{1,0:T(1,128)S(1)} %copy-done.3, s32[1,6]{1,0:T(1,128)S(1)} %copy-done.4, f32[1,3,24]{2,1,0:T(4,128)S(1)} %copy.7.inverse, f32[3,32,1024]{2,1,0:T(8,128)S(1)} %bitcast.5, s32[32,1024]{1,0:T(8,128)S(1)} %bitcast.7, f32[3,32,1024]{2,1,0:T(8,128)S(1)} %bitcast.6), custom_call_target="tpu_custom_call" | custom-call | tf_op jit(solution)/shard_map/pallas_call | solution.py:360
  61.4 0.7 %copy.9 = f32[1,3,32,1024]{3,2,1,0:T(8,128)} copy(f32[1,3,32,1024]{3,2,1,0:T(8,128)S(1)} %bitcast.4) | data formatting | bytes 786432
  (1 shorter events, 0.0 us)
Async XLA Ops:
  0.0 0.7 %copy-start.5 = (f32[1,3,24]{2,0,1:T(1,128)S(1)}, f32[1,3,24]{2,0,1:T(1,128)}, u32[]{:S(2)}) copy-start(f32[1,3,24]{2,0,1:T(1,128)} %param.11) | copy-start | bytes 868
  0.7 0.7 %copy-start.3 = (s32[1,3]{1,0:T(1,128)S(1)}, s32[1,3]{1,0:T(1,128)}, u32[]{:S(2)}) copy-start(s32[1,3]{1,0:T(1,128)} %coords.1) | copy-start | bytes 40
  0.7 0.7 %copy-start.4 = (s32[1,6]{1,0:T(1,128)S(1)}, s32[1,6]{1,0:T(1,128)}, u32[]{:S(2)}) copy-start(s32[1,6]{1,0:T(1,128)} %links.1) | copy-start | bytes 76
  1.4 1.0 %copy-start = (f32[1,3,32,1024]{3,2,1,0:T(8,128)S(1)}, f32[1,3,32,1024]{3,2,1,0:T(8,128)}, u32[]{:S(2)}) copy-start(f32[1,3,32,1024]{3,2,1,0:T(8,128)} %param.6) | copy-start | bytes 1179652
  2.3 1.0 %copy-start.1 = (f32[1,3,32,1024]{3,2,1,0:T(8,128)S(1)}, f32[1,3,32,1024]{3,2,1,0:T(8,128)}, u32[]{:S(2)}) copy-start(f32[1,3,32,1024]{3,2,1,0:T(8,128)} %param.10) | copy-start | bytes 1179652
  3.3 0.9 %copy-start.2 = (s32[1,32,1024]{2,1,0:T(8,128)S(1)}, s32[1,32,1024]{2,1,0:T(8,128)}, u32[]{:S(2)}) copy-start(s32[1,32,1024]{2,1,0:T(8,128)} %param.7) | copy-start | bytes 393220
where the time goes:
time: 62.4 us; the launch traced here: 62.1 us
  Pallas kernels  57.1 us (92%)
  local copies, waits for them, and re-layouts  4.99 us (8%)
    pallas_call x1, Pallas kernels, shards(): pl.pallas_call(functools.partial(kernel, n, m), out_shape=jax.ShapeDtypeS...  57.1 us
    unnamed x14, local copies, waits for them, and re-layouts  4.99 us

commit v1 on v0

--- a/solution.py
+++ b/solution.py
@@ -29,7 +29,8 @@
 
 def kernel(
     n, m,
-    coords, links, inverse, state_in, phase_in, source_in, out,
+    coords_in, links_in, inverse_in, state_hbm, phase_hbm, source_hbm, out,
+    coords, links, inverse, state_in, phase_in, source_in, fetch,
     state, upd, base, gain, mix, diag, source, phase,
     send, recv, squares_a, squares_b, coarse, weights,
     face_send, face_recv, a_send, a_recv, b_send, b_recv, c_send, c_recv,
@@ -44,6 +45,16 @@
     edge = first | last
     even = lane % 2 == 0
 
+    fetches = [
+        pltpu.make_async_copy(a, b, fetch.at[i])
+        for i, (a, b) in enumerate((
+            (state_hbm, state_in), (coords_in, coords), (links_in, links),
+            (phase_hbm, phase_in), (source_hbm, source_in), (inverse_in, inverse),
+        ))
+    ]
+    for copy in fetches:
+        copy.start()
+
     targets = (("space", me_s, 1, n), ("space", me_s, -1, n), ("group", me_g, 1, m), ("group", me_g, -1, m))
 
     def has(axis, me, step, size):
@@ -65,14 +76,14 @@
         axis, me, step, size = targets[d]
         return has(axis, me, -step, size)
 
-    def start_faces(r):
-        for d in range(4):
+    def start_faces(r, which):
+        for d in which:
             @pl.when(has(*targets[d]))
             def _():
                 face_copy(r, d).start()
 
-    def wait_faces(r):
-        for d in range(4):
+    def wait_faces(r, which):
+        for d in which:
             @pl.when(source_of(d))
             def _():
                 face_copy(r, d).wait_recv()
@@ -114,6 +125,8 @@
                 tiles[4 * h + r] = got[r]
         return tiles
 
+    fetches[1].wait()
+    fetches[2].wait()
     occupied = coords[0, 0] >= 0
     mask = jnp.where(occupied, 1.0, 0.0).astype(F32)
     wall = coords[0, 0].astype(F32) + coords[0, 1].astype(F32) / n + coords[0, 2].astype(F32) / m - 1.0
@@ -128,6 +141,7 @@
             for b in range(2):
                 upd[b, f, t, 0:PAD] = zero_rows
                 upd[b, f, t, PAD + E:] = zero_rows
+    fetches[0].wait()
     for f in range(3):
         tiles = spread_in(lambda t: state_in[f, :, t * 128:(t + 1) * 128])
         for t in range(TILES):
@@ -138,33 +152,46 @@
         part = roll(jnp.where(edge, c, 0.0), j)
         planes[q] = part if planes[q] is None else planes[q] + part
 
-    def post_faces(r, planes, ends):
-        q0, q1 = planes
-        send[r, 3] = jnp.where(even, q0, roll(q1, 1))
-        send[r, 2] = jnp.where(even, roll(q1, -1), q0)
+    def post_y(r, ends):
         up = jnp.where(block == 0, roll(ends[0][1], -96), jnp.where(block == 1, roll(ends[1][1], -64), roll(ends[2][1], -32)))
         down = jnp.where(block == 0, ends[0][0], jnp.where(block == 1, roll(ends[1][0], 32), roll(ends[2][0], 64)))
         send[r, 0] = up
         send[r, 1] = down
-        start_faces(r)
-
-    def ghosts_of(r, walls):
-        wait_faces(r)
-        got = [recv[r, d] for d in range(4)]
-        y_low, y_high, z_low, z_high = got
-        if walls:
-            plain = [jnp.where(linked[d], got[d], 0.0) for d in range(4)]
-            solid = [jnp.where(linked[d], got[d], wall) for d in range(4)]
-        else:
-            plain = solid = got
-        c0 = jnp.where(even, plain[3], roll(plain[2], 66))
-        c1 = jnp.where(even, roll(solid[3], -1), roll(solid[2], 67))
-        lows = [roll((plain if f < 2 else solid)[0], -32 * f) for f in range(3)]
-        highs = [roll((plain if f < 2 else solid)[1], 96 - 32 * f) for f in range(3)]
-        return (c0, c1), lows, highs
+        start_faces(r, (0, 1))
+
+    def post_z(r, planes):
+        q0, q1 = planes
+        send[r, 3] = jnp.where(even, q0, roll(q1, 1))
+        send[r, 2] = jnp.where(even, roll(q1, -1), q0)
+        start_faces(r, (2, 3))
+
+    def walled(r, d, walls):
+        got = recv[r, d]
+        if not walls:
+            return got, got
+        return jnp.where(linked[d], got, 0.0), jnp.where(linked[d], got, wall)
+
+    def ghosts_z(r, walls):
+        wait_faces(r, (2, 3))
+        low, solid_low = walled(r, 2, walls)
+        high, solid_high = walled(r, 3, walls)
+        c0 = jnp.where(even, high, roll(low, 66))
+        c1 = jnp.where(even, roll(solid_high, -1), roll(solid_low, 67))
+        return c0, c1
+
+    def ghosts_y(r, walls):
+        wait_faces(r, (0, 1))
+        low = walled(r, 0, walls)
+        high = walled(r, 1, walls)
+        lows = [roll(low[f // 2], -32 * f) for f in range(3)]
+        highs = [roll(high[f // 2], 96 - 32 * f) for f in range(3)]
+        return lows, highs
+
+    inside = tuple(range(1, TILES - 1))
+    outside = (0, TILES - 1)
 
     def around(ref, f, t, ghosts):
-        planes, lows, highs = ghosts
+        planes, (lows, highs) = ghosts
         c = ref[f, t, PAD:PAD + E]
         total = ref[f, t, PAD - 1:PAD - 1 + E] + ref[f, t, PAD + 1:PAD + 1 + E]
         if t > 0:
@@ -180,17 +207,19 @@
         total = total + jnp.where(last, ghost, roll(c, -1)) + jnp.where(first, ghost, roll(c, 1))
         return c, total
 
-    def post_state(r):
+    def pack_state():
         planes, ends = [None, None], []
         for f in range(3):
             tiles = [state[f, t, PAD:PAD + E] for t in range(TILES)]
             for t in range(TILES):
                 pack_z(planes, f, t, tiles[t])
             ends.append((tiles[0], tiles[TILES - 1]))
-        post_faces(r, planes, ends)
-
+        return planes, ends
+
+    planes, ends = pack_state()
     pl.semaphore_wait(barrier, n + m - 2)
-    post_state(0)
+    post_y(0, ends)
+    post_z(0, planes)
 
     rows8 = lax.broadcasted_iota(jnp.int32, (8, 128), 0)
     blank = jnp.zeros((E, 128), F32)
@@ -199,6 +228,8 @@
         def _():
             for r in range(NEWTON * ROUNDS):
                 recv[r, d] = blank
+    for copy in fetches[3:]:
+        copy.wait()
     for f in range(3):
         tiles = spread_in(lambda t: source_in[f, :, t * 128:(t + 1) * 128])
         for t in range(TILES):
@@ -209,7 +240,7 @@
     for d in range(n):
         owner = lax.rem(me_s - d + n, n)
         for i in range(3):
-            v = [inverse[0, i, 3 * owner + f] for f in range(3)]
+            v = [inverse[i, 0, 3 * owner + f] for f in range(3)]
             weights[i, d] = jnp.where(rows8 == 0, v[0], jnp.where(rows8 == 1, v[1], jnp.where(rows8 == 2, v[2], 0.0)))
 
     def fold(x):
@@ -217,10 +248,13 @@
 
     def sweep(k, carry):
         r0 = k * ROUNDS
-        ghosts = ghosts_of(r0, True)
+        planes_in = ghosts_z(r0, True)
+        ghosts = (planes_in, (None, None))
         planes, ends = [None, None], [[None, None] for _ in range(3)]
         square = jnp.zeros((E, 128), F32)
-        for t in range(TILES):
+        for t in inside + outside:
+            if t == 0:
+                ghosts = (planes_in, ghosts_y(r0, True))
             label = phase[t]
             pore = label == 0
             active = label == 1
@@ -252,7 +286,8 @@
                     ends[f][0] = b
                 if t == TILES - 1:
                     ends[f][1] = b
-        post_faces(r0 + 1, planes, ends)
+        post_y(r0 + 1, ends)
+        post_z(r0 + 1, planes)
         squares_a[k, 0] = fold(square)
         gather_start(over_a, k, "space", me_s, n)
 
@@ -266,9 +301,12 @@
         def smooth(p, carry):
             now = lax.rem(p, 2)
             u, later = upd.at[now], upd.at[1 - now]
-            ghosts = ghosts_of(r0 + 1 + p, False)
+            planes_in = ghosts_z(r0 + 1 + p, False)
+            ghosts = (planes_in, (None, None))
             planes, ends = [None, None], [[None, None] for _ in range(3)]
-            for t in range(TILES):
+            for t in inside + outside:
+                if t == 0:
+                    ghosts = (planes_in, ghosts_y(r0 + 1 + p, False))
                 for f, (v, term) in enumerate(terms(u, t, ghosts)):
                     value = (1.0 - OMEGA) * v + term
                     later[f, t, PAD:PAD + E] = value
@@ -277,7 +315,8 @@
                         ends[f][0] = value
                     if t == TILES - 1:
                         ends[f][1] = value
-            post_faces(r0 + 2 + p, planes, ends)
+            post_y(r0 + 2 + p, ends)
+            post_z(r0 + 2 + p, planes)
             return carry
 
         lax.fori_loop(0, 1, smooth, 0)
@@ -290,9 +329,12 @@
         lax.fori_loop(1, SMOOTH - 1, smooth, 0)
 
         u = upd.at[(SMOOTH - 1) % 2]
-        ghosts = ghosts_of(r0 + SMOOTH, False)
+        planes_in = ghosts_z(r0 + SMOOTH, False)
+        ghosts = (planes_in, (None, None))
         sums = [jnp.zeros((E, 128), F32) for _ in range(3)]
-        for t in range(TILES):
+        for t in inside + outside:
+            if t == 0:
+                ghosts = (planes_in, ghosts_y(r0 + SMOOTH, False))
             for f, (v, term) in enumerate(terms(u, t, ghosts)):
                 sums[f] = sums[f] + diag[f, t] * (term - OMEGA * v)
         rows = [jnp.sum(x, axis=0, keepdims=True) for x in sums]
@@ -326,7 +368,8 @@
 
         @pl.when(k < NEWTON - 1)
         def _():
-            post_faces(r0 + ROUNDS, planes, ends)
+            post_y(r0 + ROUNDS, ends)
+            post_z(r0 + ROUNDS, planes)
 
         return carry
 
@@ -352,7 +395,7 @@
 
 def shards(n, m, initial_state, phases, brick_coords, neighbours, source, coarse_inverse):
     rounds = NEWTON * ROUNDS
-    smem = pl.BlockSpec(memory_space=pltpu.SMEM)
+    anywhere = pl.BlockSpec(memory_space=pl.ANY)
     vmem = pl.BlockSpec(memory_space=pltpu.VMEM)
     padded = (3, TILES, E + 2 * PAD, 128)
     inner = (3, TILES, E, 128)
@@ -360,9 +403,16 @@
     result = pl.pallas_call(
         functools.partial(kernel, n, m),
         out_shape=jax.ShapeDtypeStruct((3, E, E * E), F32),
-        in_specs=[smem, smem, smem, vmem, vmem, vmem],
+        in_specs=[anywhere] * 6,
         out_specs=vmem,
         scratch_shapes=[
+            pltpu.SMEM((1, 3), jnp.int32),
+            pltpu.SMEM((1, 6), jnp.int32),
+            pltpu.SMEM((3, 1, 3 * n), F32),
+            pltpu.VMEM((3, E, E * E), F32),
+            pltpu.VMEM((E, E * E), jnp.int32),
+            pltpu.VMEM((3, E, E * E), F32),
+            dma((6,)),
             pltpu.VMEM(padded, F32),
             pltpu.VMEM((2,) + padded, F32),
             pltpu.VMEM(inner, F32),
@@ -383,9 +433,9 @@
             dma((NEWTON, n)), dma((NEWTON, n)),
         ],
         compiler_params=pltpu.CompilerParams(
-            collective_id=0, has_side_effects=True, vmem_limit_bytes=40 * 1024 * 1024
+            collective_id=0, has_side_effects=True, vmem_limit_bytes=56 * 1024 * 1024
         ),
-    )(brick_coords, neighbours, coarse_inverse, initial_state[0], phases[0], source[0])
+    )(brick_coords, neighbours, jnp.swapaxes(coarse_inverse, 0, 1), initial_state[0], phases[0], source[0])
     return result[None]
 
 

time: 62.4 us -> 53.7 us (0.86)
  Pallas kernels: 57.1 us -> 51.7 us
  local copies, waits for them, and re-layouts: 4.99 us -> 1.77 us
    pallas_call x1, Pallas kernels: 57.1 us -> 51.7 us  [shards(): pl.pallas_call(functools.partial(kernel, n, m), out_shape=jax.ShapeDtypeS...]
    unnamed x14 -> x1, local copies, waits for them, and re-layouts: 4.99 us -> 1.77 us
where the time goes in v1:
time: 53.7 us; the launch traced here: 53.5 us
  Pallas kernels  51.7 us (96%)
  local copies, waits for them, and re-layouts  1.77 us (3%)
    pallas_call x1, Pallas kernels, shards(): pl.pallas_call(functools.partial(kernel, n, m), out_shape=jax.ShapeDtypeS...  51.7 us
    unnamed x1, local copies, waits for them, and re-layouts  1.77 us

profile of v1, /device:TPU:0, one launch (start us, length us, event | category | flops | bytes accessed | tf_op | source)
XLA Modules:
  0.0 53.5 jit_solution(2547633278096462423)
XLA Ops:
  0.0 51.7 %shard_map.64 = f32[3,32,1024]{2,1,0:T(8,128)} custom-call(s32[1,3]{1,0:T(1,128)} %coords_in.1, s32[1,6]{1,0:T(1,128)} %links_in.1, f32[3,1,24]{2,1,0:T(1,128)} %bitcast.9, f32[3,32,1024]{2,1,0:T(8,128)} %bitcast.6, s32[32,1024]{1,0:T(8,128)} %bitcast.8, f32[3,32,1024]{2,1,0:T(8,128)} %bitcast.7), custom_call_target="tpu_custom_call" | custom-call | tf_op jit(solution)/shard_map/pallas_call | solution.py:403
  51.8 1.8 %copy.8 = f32[1,3,32,1024]{3,2,1,0:T(8,128)} copy(f32[1,3,32,1024]{3,2,1,0:T(8,128)} %bitcast.5) | data formatting | bytes 786432

commit v2 on v1

--- a/solution.py
+++ b/solution.py
@@ -152,17 +152,21 @@
         part = roll(jnp.where(edge, c, 0.0), j)
         planes[q] = part if planes[q] is None else planes[q] + part
 
-    def post_y(r, ends):
+    def y_planes(ends):
         up = jnp.where(block == 0, roll(ends[0][1], -96), jnp.where(block == 1, roll(ends[1][1], -64), roll(ends[2][1], -32)))
         down = jnp.where(block == 0, ends[0][0], jnp.where(block == 1, roll(ends[1][0], 32), roll(ends[2][0], 64)))
-        send[r, 0] = up
-        send[r, 1] = down
+        return [up, down]
+
+    def z_planes(planes):
+        q0, q1 = planes
+        return [jnp.where(even, roll(q1, -1), q0), jnp.where(even, q0, roll(q1, 1))]
+
+    def post_y(r, ends):
+        send[r, 0], send[r, 1] = y_planes(ends)
         start_faces(r, (0, 1))
 
     def post_z(r, planes):
-        q0, q1 = planes
-        send[r, 3] = jnp.where(even, q0, roll(q1, 1))
-        send[r, 2] = jnp.where(even, roll(q1, -1), q0)
+        send[r, 2], send[r, 3] = z_planes(planes)
         start_faces(r, (2, 3))
 
     def walled(r, d, walls):
@@ -349,38 +353,51 @@
         cells = 3.0 * n * m * E * E * E
         damping = 1.0 / (1.0 + jnp.sqrt(whole / cells + 1e-6))
 
+        planes, ends = [None, None], []
+        for f in range(3):
+            tiles = []
+            for t in range(TILES):
+                value = state[f, t, PAD:PAD + E] + damping * u[f, t, PAD:PAD + E]
+                state[f, t, PAD:PAD + E] = value
+                pack_z(planes, f, t, value)
+                tiles.append(value)
+            ends.append((tiles[0], tiles[TILES - 1]))
+            for h in range(2):
+                got = swap4(tiles[4 * h:4 * h + 4])
+                for q in range(4):
+                    t = 2 * q + h
+                    out[f, :, t * 128:(t + 1) * 128] = got[q]
+        pack = y_planes(ends) + z_planes(planes)
+
         gather_wait(over_c, k, "space", me_s, n)
         got = [coarse[k, d] for d in range(n)]
-        planes, ends = [None, None], [[None, None] for _ in range(3)]
+        lifts = []
         for f in range(3):
             acc = got[0] * weights[f, 0]
             for d in range(1, n):
                 acc = acc + got[d] * weights[f, d]
-            lift = mask * jnp.sum(jnp.sum(acc, axis=0, keepdims=True), axis=1, keepdims=True)
-            for t in range(TILES):
-                value = state[f, t, PAD:PAD + E] + damping * (u[f, t, PAD:PAD + E] + lift)
-                state[f, t, PAD:PAD + E] = value
-                pack_z(planes, f, t, value)
-                if t == 0:
-                    ends[f][0] = value
-                if t == TILES - 1:
-                    ends[f][1] = value
+            lifts.append(damping * (mask * jnp.sum(jnp.sum(acc, axis=0, keepdims=True), axis=1, keepdims=True)))
 
         @pl.when(k < NEWTON - 1)
         def _():
-            post_y(r0 + ROUNDS, ends)
-            post_z(r0 + ROUNDS, planes)
+            by_block = jnp.where(block == 0, lifts[0], jnp.where(block == 1, lifts[1], lifts[2]))
+            below = jnp.where(even, lifts[2], jnp.where((depth < 15) | last, lifts[0], lifts[1]))
+            above = jnp.where(even, jnp.where(depth < 16, lifts[0], lifts[1]), lifts[2])
+            for d, part in enumerate((by_block, by_block, below, above)):
+                send[r0 + ROUNDS, d] = pack[d] + part
+            start_faces(r0 + ROUNDS, (0, 1, 2, 3))
+            for f in range(3):
+                for t in range(TILES):
+                    state[f, t, PAD:PAD + E] = state[f, t, PAD:PAD + E] + lifts[f]
+
+        @pl.when(k == NEWTON - 1)
+        def _():
+            for f in range(3):
+                out[f] = out[f] + lifts[f]
 
         return carry
 
     lax.fori_loop(0, NEWTON, sweep, 0)
-
-    for f in range(3):
-        for h in range(2):
-            got = swap4([state[f, 4 * h + r, PAD:PAD + E] for r in range(4)])
-            for k in range(4):
-                t = 2 * k + h
-                out[f, :, t * 128:(t + 1) * 128] = got[k]
 
     for r in range(NEWTON * ROUNDS):
         for d in range(4):

time: 53.7 us -> 52.9 us (0.985)
  Pallas kernels: 51.7 us -> 50.9 us
    pallas_call x1, Pallas kernels: 51.7 us -> 50.9 us  [shards(): pl.pallas_call(functools.partial(kernel, n, m), out_shape=jax.ShapeDtypeS...]
where the time goes in v2:
time: 52.9 us; the launch traced here: 52.7 us
  Pallas kernels  50.9 us (96%)
  local copies, waits for them, and re-layouts  1.77 us (3%)
    pallas_call x1, Pallas kernels, shards(): pl.pallas_call(functools.partial(kernel, n, m), out_shape=jax.ShapeDtypeS...  50.9 us
    unnamed x1, local copies, waits for them, and re-layouts  1.77 us

profile of v2, /device:TPU:0, one launch (start us, length us, event | category | flops | bytes accessed | tf_op | source)
XLA Modules:
  0.0 52.7 jit_solution(10029664425644694863)
XLA Ops:
  0.0 50.9 %shard_map.64 = f32[3,32,1024]{2,1,0:T(8,128)} custom-call(s32[1,3]{1,0:T(1,128)} %coords_in.1, s32[1,6]{1,0:T(1,128)} %links_in.1, f32[3,1,24]{2,1,0:T(1,128)} %bitcast.9, f32[3,32,1024]{2,1,0:T(8,128)} %bitcast.6, s32[32,1024]{1,0:T(8,128)} %bitcast.8, f32[3,32,1024]{2,1,0:T(8,128)} %bitcast.7), custom_call_target="tpu_custom_call" | custom-call | tf_op jit(solution)/shard_map/pallas_call | solution.py:420
  50.9 1.8 %copy.8 = f32[1,3,32,1024]{3,2,1,0:T(8,128)} copy(f32[1,3,32,1024]{3,2,1,0:T(8,128)} %bitcast.5) | data formatting | bytes 786432

commit v3 on v2

--- a/solution.py
+++ b/solution.py
@@ -302,24 +302,36 @@
             cross = (s - e, s - half, e + half)
             return [(pairs[f][0], base[f, t] + gain[f, t] * pairs[f][1] + mix[f, t] * cross[f]) for f in range(3)]
 
+        no_y = ([0.0] * 3, [0.0] * 3)
+
+        def y_extras(r):
+            lows, highs = ghosts_y(r, False)
+            for f in range(3):
+                yield f, 0, gain[f, 0] * jnp.where(block == 0, lows[f], 0.0)
+                yield f, TILES - 1, gain[f, TILES - 1] * jnp.where(block == 3, highs[f], 0.0)
+
         def smooth(p, carry):
             now = lax.rem(p, 2)
             u, later = upd.at[now], upd.at[1 - now]
-            planes_in = ghosts_z(r0 + 1 + p, False)
-            ghosts = (planes_in, (None, None))
+            ghosts = (ghosts_z(r0 + 1 + p, False), no_y)
+            parts = {}
             planes, ends = [None, None], [[None, None] for _ in range(3)]
             for t in inside + outside:
-                if t == 0:
-                    ghosts = (planes_in, ghosts_y(r0 + 1 + p, False))
                 for f, (v, term) in enumerate(terms(u, t, ghosts)):
                     value = (1.0 - OMEGA) * v + term
+                    if t in outside:
+                        parts[f, t] = value
+                    else:
+                        later[f, t, PAD:PAD + E] = value
+                        pack_z(planes, f, t, value)
+            for f, t, extra in y_extras(r0 + 1 + p):
+                ends[f][t // (TILES - 1)] = parts[f, t] + extra
+            post_y(r0 + 2 + p, ends)
+            for f in range(3):
+                for t in outside:
+                    value = ends[f][t // (TILES - 1)]
                     later[f, t, PAD:PAD + E] = value
                     pack_z(planes, f, t, value)
-                    if t == 0:
-                        ends[f][0] = value
-                    if t == TILES - 1:
-                        ends[f][1] = value
-            post_y(r0 + 2 + p, ends)
             post_z(r0 + 2 + p, planes)
             return carry
 
@@ -333,14 +345,13 @@
         lax.fori_loop(1, SMOOTH - 1, smooth, 0)
 
         u = upd.at[(SMOOTH - 1) % 2]
-        planes_in = ghosts_z(r0 + SMOOTH, False)
-        ghosts = (planes_in, (None, None))
+        ghosts = (ghosts_z(r0 + SMOOTH, False), no_y)
         sums = [jnp.zeros((E, 128), F32) for _ in range(3)]
         for t in inside + outside:
-            if t == 0:
-                ghosts = (planes_in, ghosts_y(r0 + SMOOTH, False))
             for f, (v, term) in enumerate(terms(u, t, ghosts)):
                 sums[f] = sums[f] + diag[f, t] * (term - OMEGA * v)
+        for f, t, extra in y_extras(r0 + SMOOTH):
+            sums[f] = sums[f] + diag[f, t] * extra
         rows = [jnp.sum(x, axis=0, keepdims=True) for x in sums]
         coarse[k, 0] = jnp.where(rows8 == 0, rows[0], jnp.where(rows8 == 1, rows[1], jnp.where(rows8 == 2, rows[2], 0.0)))
         gather_start(over_c, k, "space", me_s, n)

time: 52.9 us -> 52.2 us (0.987)
  Pallas kernels: 50.9 us -> 50.3 us
    pallas_call x1, Pallas kernels: 50.9 us -> 50.3 us  [shards(): pl.pallas_call(functools.partial(kernel, n, m), out_shape=jax.ShapeDtypeS...]
where the time goes in v3:
time: 52.2 us; the launch traced here: 52.1 us
  Pallas kernels  50.3 us (96%)
  local copies, waits for them, and re-layouts  1.77 us (3%)
    pallas_call x1, Pallas kernels, shards(): pl.pallas_call(functools.partial(kernel, n, m), out_shape=jax.ShapeDtypeS...  50.3 us
    unnamed x1, local copies, waits for them, and re-layouts  1.77 us

profile of v3, /device:TPU:0, one launch (start us, length us, event | category | flops | bytes accessed | tf_op | source)
XLA Modules:
  0.0 52.1 jit_solution(11941513343259416779)
XLA Ops:
  0.0 50.3 %shard_map.64 = f32[3,32,1024]{2,1,0:T(8,128)} custom-call(s32[1,3]{1,0:T(1,128)} %coords_in.1, s32[1,6]{1,0:T(1,128)} %links_in.1, f32[3,1,24]{2,1,0:T(1,128)} %bitcast.9, f32[3,32,1024]{2,1,0:T(8,128)} %bitcast.6, s32[32,1024]{1,0:T(8,128)} %bitcast.8, f32[3,32,1024]{2,1,0:T(8,128)} %bitcast.7), custom_call_target="tpu_custom_call" | custom-call | tf_op jit(solution)/shard_map/pallas_call | solution.py:431
  50.3 1.8 %copy.8 = f32[1,3,32,1024]{3,2,1,0:T(8,128)} copy(f32[1,3,32,1024]{3,2,1,0:T(8,128)} %bitcast.5) | data formatting | bytes 786432
